TPU v7x, 32 devices: a whole 2x2x4 slice. The times are simulated.
32 devices in a mesh: groups: 2 (over y), traj: 16 (over z, x, core).
Axes of the slice: x: 2, y: 2, z: 4, core: 2. Of those that a mesh axis runs over, the one named last changes fastest.
Arguments:
- trajectories: bfloat16 [16384, 192], P(('groups', 'traj')), parts along dimension 0
- landmark_index: int32 [1024], P(('groups', 'traj')), parts along dimension 0, may hold values from 0 to 8191, as said below
- start_vectors: float32 [16384, 32], P(('groups', 'traj')), parts along dimension 0, may hold values from -6 to 6
Outputs:
- embedding: float32 [16384, 32], P(('groups', 'traj')), parts along dimension 0
There are 2 independent parts, one for each index of `groups`. A program takes and returns all parts, laid end to end along the dimension named above; each array names one. Nothing has to cross between parts.
Inputs may be any that keep to these rules, and one draw needn't show every extreme that they name: `landmark_index`: entries b * 32 to (b + 1) * 32 - 1 are distinct rows of the range b * 512 to (b + 1) * 512 - 1, for every b.
All inputs are finite; a program needn't handle non-finite values.
Results may differ from a plain program's by a relative error of at most 0.0003.
Values may be sent and summed in bfloat16 or wider, within the bound.
A program may use at most 64 MiB of HBM per device.

v0:
```python
import math
import jax
import jax.numpy as jnp
from jax import lax
from jax.sharding import PartitionSpec as P

SWEEPS = 2
HIGH = lax.Precision.HIGHEST


def kernel_turned(rows, row_norms, lands):
    wide = lands.astype(jnp.float32)
    land_norms = jnp.sum(wide * wide, axis=1)
    cross = lax.dot_general(
        lands, rows, (((1,), (1,)), ((), ())), preferred_element_type=jnp.float32
    )
    dist = land_norms[:, None] + row_norms[None, :] - 2.0 * cross
    return jnp.exp(-dist * (2.0 / rows.shape[1]))


def column_fold(rows, row_norms, weighted):

    def fold(total, piece, start):
        count = piece.shape[0]
        width = math.gcd(count, 512)

        def step_block(j, acc):
            lands = lax.dynamic_slice_in_dim(piece, j * width, width, 0)
            block = kernel_turned(rows, row_norms, lands)
            part = jnp.dot(block, weighted, precision=HIGH, preferred_element_type=jnp.float32)
            return lax.dynamic_update_slice_in_dim(acc, part, j * width, 0)

        return lax.fori_loop(0, count // width, step_block, total)

    return fold


def row_fold(rows, row_norms, mixing):

    def fold(total, piece, start):
        count = piece.shape[0]
        width = math.gcd(count, 512)

        def step_block(j, acc):
            lands = lax.dynamic_slice_in_dim(piece, j * width, width, 0)
            block = kernel_turned(rows, row_norms, lands)
            mix = lax.dynamic_slice_in_dim(mixing, j * width, width, 0)
            return acc + lax.dot_general(
                block,
                mix,
                (((0,), (0,)), ((), ())),
                precision=HIGH,
                preferred_element_type=jnp.float32,
            )

        return lax.fori_loop(0, count // width, step_block, total)

    return fold


def over_columns(rows, row_norms, weighted, own_lands):
    total_lands = own_lands.shape[0] * lax.axis_size("traj")
    start = jnp.zeros((total_lands, weighted.shape[1]), jnp.float32)
    fold = column_fold(rows, row_norms, weighted)
    return fold(start, lax.all_gather(own_lands, "traj", axis=0, tiled=True), jnp.int32(0))


def over_rows(rows, row_norms, mixing, own_lands):
    start = jnp.zeros((rows.shape[0], mixing.shape[1]), jnp.float32)
    fold = row_fold(rows, row_norms, mixing)
    return fold(start, lax.all_gather(own_lands, "traj", axis=0, tiled=True), jnp.int32(0))


def orthonormal(block, gram):
    lower = jnp.linalg.cholesky(gram)
    return jax.scipy.linalg.solve_triangular(lower, block.T, lower=True).T


def orthonormal_upper(block, gram):
    return orthonormal(block[:, ::-1], gram[::-1, ::-1])[:, ::-1]


def landmark_reduce(partial_value, scale_all):
    total = lax.psum(partial_value, "traj")
    return total / scale_all


def local(trajectories, landmark_index, start_vectors):
    row_dev = trajectories.shape[0]
    wide_rows = trajectories.astype(jnp.float32)
    row_norms = jnp.sum(wide_rows * wide_rows, axis=1)
    local_index = landmark_index - lax.axis_index("traj") * row_dev
    own_lands = jnp.take(trajectories, local_index, axis=0)
    own_norms = jnp.take(row_norms, local_index, axis=0)
    total_lands = own_lands.shape[0] * lax.axis_size("traj")
    land_deg = over_rows(own_lands, own_norms, jnp.ones((total_lands, 1), jnp.float32), own_lands)
    deg_all = lax.all_gather(land_deg, "traj", axis=0, tiled=True)
    col_part = over_columns(trajectories, row_norms, jnp.ones((row_dev, 1), jnp.float32), own_lands)
    ratio = landmark_reduce(col_part, deg_all)
    degree = over_rows(trajectories, row_norms, ratio, own_lands)
    dinv = lax.rsqrt(degree)
    vectors = start_vectors
    gram_part = None
    for sweep in range(SWEEPS):
        if gram_part is not None:
            gram = lax.psum(gram_part, "traj")
            vectors = orthonormal_upper(vectors, gram)
        partial_value = over_columns(trajectories, row_norms, dinv * vectors, own_lands)
        scaled = landmark_reduce(partial_value, deg_all)
        vectors = dinv * over_rows(trajectories, row_norms, scaled, own_lands)
        gram_part = jnp.dot(vectors.T, vectors, precision=HIGH, preferred_element_type=jnp.float32)
    gram = lax.psum(gram_part, "traj")
    vectors = orthonormal(vectors, gram)
    return math.sqrt(row_dev * lax.axis_size("traj")) * vectors


def solution(mesh):
    return jax.shard_map(
        local,
        mesh=mesh,
        in_specs=(P(("groups", "traj"), None), P(("groups", "traj")), P(("groups", "traj"), None)),
        out_specs=P(("groups", "traj"), None),
        check_vma=False,
    )
```

profile of v0, /device:TPU:0, one launch (start us, length us, event | category | flops | bytes accessed | tf_op | source)
XLA Modules:
  0.0 389.3 jit_solution(15879041102556417802)
XLA Ops:
  6.5 1.1 multiply_reduce_fusion.1
  7.8 0.6 copy-done.2
  8.4 0.7 gather_fusion.1
  9.8 23.8 %all_gather.4 = bf16[512,192]{1,0:T(8,128)(2,1)S(1)} all-gather(bf16[32,192]{1,0:T(8,128)(2,1)S(1)} %broadcast_select_fusion), channel_id=1, replica_groups=mesh['groups'=2,'traj'=16] {'traj'}, dimensions={0}, use_global_device_ids=true | all-gather | bytes 208896 | tf_op jit(solution)/shard_map/all_gather | solution.py:71
  34.6 1.0 convolution_bitcast_fusion.1
  37.1 29.8 %all-reduce.1 = (f32[512,1]{0,1:T(1,128)S(1)}, f32[512]{0:T(512)S(1)}) all-reduce(f32[512,1]{0,1:T(1,128)S(1)} %convolution_bitcast_fusion.1, f32[512]{0:T(512)S(1)} %dynamic-update-slice.2), channel_id=1, replica_groups=mesh['groups'=2,'traj'=16] {'traj'}, use_global_device_ids=true, to_apply=%region_2.3 | all-reduce | flops 1024 | bytes 8192 | tf_op jit(solution)/shard_map/psum | solution.py:84
  66.9 0.7 fusion.29
  67.8 1.7 fusion.17
  69.5 86.2 %all-reduce.5.cloned.1.call-done = f32[512,32]{1,0:T(8,128)} async-done(((f32[512,32]{1,0:T(8,128)}), f32[512,32]{1,0:T(8,128)}) %all-reduce.5.cloned.1.call-update) | async-done | bytes 65552 | tf_op jit(solution)/shard_map/psum | solution.py:84
  155.7 1.7 convolution_multiply_fusion.4
  157.8 60.0 %psum.37 = f32[32,32]{0,1:T(8,128)S(1)} all-reduce(f32[32,32]{0,1:T(8,128)S(1)} %rev.9), channel_id=1, replica_groups=mesh['groups'=2,'traj'=16] {'traj'}, use_global_device_ids=true, to_apply=%region_4.5 | all-reduce | flops 1024 | bytes 8192 | tf_op jit(solution)/shard_map/psum | solution.py:106
  217.9 2.9 cholesky.44
  220.9 0.6 compare_reduce_fusion.1
  221.5 0.7 fusion.21
  222.2 2.5 custom-call.6
  225.0 1.7 fusion.15
  226.7 86.2 %all-reduce.7.cloned.1.call-done = f32[512,32]{1,0:T(8,128)} async-done(((f32[512,32]{1,0:T(8,128)}), f32[512,32]{1,0:T(8,128)}) %all-reduce.7.cloned.1.call-update) | async-done | bytes 65552 | tf_op jit(solution)/shard_map/psum | solution.py:84
  312.9 1.7 convolution_multiply_fusion.3
  314.8 60.0 %psum.39 = f32[32,32]{0,1:T(8,128)S(1)} all-reduce(f32[32,32]{0,1:T(8,128)S(1)} %fusion.36), channel_id=1, replica_groups=mesh['groups'=2,'traj'=16] {'traj'}, use_global_device_ids=true, to_apply=%region_8.11 | all-reduce | flops 1024 | bytes 8192 | tf_op jit(solution)/shard_map/psum | solution.py:112
  374.9 2.9 cholesky.55
  377.8 0.6 compare_reduce_fusion
  378.5 0.7 fusion.22
  379.1 2.4 custom-call.7
  381.6 0.9 fusion.8
  (37 shorter events, 4.1 us)
Async XLA Ops:
  6.5 1.1 copy-start
  6.5 149.2 %all-reduce.5.cloned.1.call-start = ((), (), s32[]{:S(2)}) async-start(), calls=%async_computation | async-start | bytes 524288 | tf_op jit(solution)/shard_map/psum | solution.py:84
  7.7 0.7 copy-start.2
  34.6 1.0 copy-start.3
  66.9 0.8 copy-start.1
  69.5 243.4 %all-reduce.7.cloned.1.call-start = ((), (), s32[]{:S(2)}) async-start(), calls=%async_computation.1 | async-start | bytes 524288 | tf_op jit(solution)/shard_map/psum | solution.py:84
Sparse Core Ops, SparseCore 0:
  69.6 86.0 all-reduce.4
  226.8 85.9 all-reduce.6
where the time goes:
time: 390 us; the launch traced here: 389 us
  blocking collectives  174 us (45%)
  waiting for transfers between devices  172 us (44%)
  other arithmetic  14.7 us (4%)
  between operations  14.2 us (4%)
  matrix products  10.9 us (3%)
    psum x2, waiting for transfers between devices, landmark_reduce(): total = lax.psum(partial_value, 'traj')  172 us
    psum x2, blocking collectives, local(): gram = lax.psum(gram_part, 'traj')  120 us
    psum x1, blocking collectives, landmark_reduce(): total = lax.psum(partial_value, 'traj')  29.8 us
    all_gather x1, blocking collectives, over_rows(): lax.all_gather(own_lands, 'traj', axis=0, tiled=True)  23.8 us
  transfers between devices with their start and end apart: 2, of which 2 were waited for; matrix products, arithmetic and copies ran while one was open for 0% of the time, Pallas kernels for 0%

commit v1 on v0

--- a/solution.py
+++ b/solution.py
@@ -6,6 +6,28 @@
 
 SWEEPS = 2
 HIGH = lax.Precision.HIGHEST
+
+
+def laid_out(pieces, dim):
+    lengths = list(pieces.shape[1:])
+    lengths[dim] *= pieces.shape[0]
+    return jnp.moveaxis(pieces, 0, dim).reshape(lengths)
+
+
+def collect(x, axis, dim):
+    size = lax.axis_size(axis)
+    pairs = [(i, (i + 1) % size) for i in range(size)]
+    back = [(b, a) for a, b in pairs]
+    lower, upper = ([], [])
+    for step in range(size - 1):
+        if step % 2 == 0:
+            lower.append(lax.ppermute(lower[-1] if lower else x, axis, pairs))
+        else:
+            upper.append(lax.ppermute(upper[-1] if upper else x, axis, back))
+    pieces = jnp.stack([*lower[::-1], x, *upper])
+    shift = lax.axis_index(axis) - len(lower)
+    pieces = pieces[(jnp.arange(size) - shift) % size]
+    return laid_out(pieces, dim)
 
 
 def kernel_turned(rows, row_norms, lands):
@@ -68,7 +90,7 @@
 def over_rows(rows, row_norms, mixing, own_lands):
     start = jnp.zeros((rows.shape[0], mixing.shape[1]), jnp.float32)
     fold = row_fold(rows, row_norms, mixing)
-    return fold(start, lax.all_gather(own_lands, "traj", axis=0, tiled=True), jnp.int32(0))
+    return fold(start, collect(own_lands, "traj", 0), jnp.int32(0))
 
 
 def orthonormal(block, gram):

time: 390 us -> 435 us (1.12)
  starting transfers between devices: 0.04 us -> 32.6 us
  waiting for transfers between devices: 172 us -> 184 us
    ppermute x0 -> x15, starting transfers between devices: none -> 32.6 us  [the longest x7 32.2 us: collect(): upper.append(lax.ppermute(upper[-1] if upper else x, axis, back))]
    ppermute x0 -> x15, waiting for transfers between devices: none -> 11.7 us  [the longest x8 7.66 us: collect(): lower.append(lax.ppermute(lower[-1] if lower else x, axis, pairs))]
    all_gather x1, blocking collectives: 23.8 us -> 18.9 us  [over_columns(): lax.all_gather(own_lands, 'traj', axis=0, tiled=True)]
  transfers between devices with their start and end apart: 2 -> 17, of which waited for: 2 -> 8; matrix products, arithmetic and copies ran while one was open for 0% -> 1% of each run, Pallas kernels for 0% -> 0%
where the time goes in v1:
time: 435 us
  waiting for transfers between devices  184 us (42%)
  blocking collectives  173 us (40%)
  starting transfers between devices  32.6 us (7%)
  between operations  14.3 us (3%)
  other arithmetic  13.9 us (3%)
  matrix products  11.2 us (3%)
  local copies, waits for them, and re-layouts  5.84 us (1%)
    psum x2, waiting for transfers between devices, landmark_reduce(): total = lax.psum(partial_value, 'traj')  172 us
    psum x2, blocking collectives, local(): gram = lax.psum(gram_part, 'traj')  120 us
    psum x1, blocking collectives, landmark_reduce(): total = lax.psum(partial_value, 'traj')  33.9 us
    ppermute x7, starting transfers between devices, collect(): upper.append(lax.ppermute(upper[-1] if upper else x, axis, back))  32.2 us
    all_gather x1, blocking collectives, over_columns(): lax.all_gather(own_lands, 'traj', axis=0, tiled=True)  18.9 us
  transfers between devices with their start and end apart: 17, of which 8 were waited for; matrix products, arithmetic and copies ran while one was open for 1% of the time, Pallas kernels for 0%

profile of v1, /device:TPU:0, one launch (start us, length us, event | category | flops | bytes accessed | tf_op | source)
XLA Modules:
  0.0 434.9 jit_solution(2853975136629767841)
XLA Ops:
  9.0 5.4 %collective-permute-start.8 = (bf16[32,192]{1,0:T(8,128)(2,1)S(1)}, bf16[32,192]{1,0:T(8,128)(2,1)S(1)}, u32[]{:S(2)}, u32[]{:S(2)}) collective-permute-start(bf16[32,192]{1,0:T(8,128)(2,1)S(1)} %broadcast_select_fusion), channel_id=1, source_target_pairs={{1,0},{2,1},{3,2},{4,3},{5,4},{6,5},{7,6},{8,7},{9,8},{10,9},{11,1... | collective-permute-start | bytes 36872 | tf_op jit(solution)/shard_map/ppermute | solution.py:26
  14.4 18.9 %all_gather.8 = bf16[512,192]{1,0:T(8,128)(2,1)S(1)} all-gather(bf16[32,192]{1,0:T(8,128)(2,1)S(1)} %broadcast_select_fusion), channel_id=1, replica_groups=mesh['groups'=2,'traj'=16] {'traj'}, dimensions={0}, use_global_device_ids=true | all-gather | bytes 208896 | tf_op jit(solution)/shard_map/all_gather | solution.py:87
  33.8 5.4 %collective-permute-done.1 = bf16[32,192]{1,0:T(8,128)(2,1)S(1)} collective-permute-done((bf16[32,192]{1,0:T(8,128)(2,1)S(1)}, bf16[32,192]{1,0:T(8,128)(2,1)S(1)}, u32[]{:S(2)}, u32[]{:S(2)}) %collective-permute-start.1) | collective-permute-done | bytes 12320 | tf_op jit(solution)/shard_map/ppermute | solution.py:24
  39.2 4.5 %collective-permute-start.9 = (bf16[32,192]{1,0:T(8,128)(2,1)S(1)}, bf16[32,192]{1,0:T(8,128)(2,1)S(1)}, u32[]{:S(2)}, u32[]{:S(2)}) collective-permute-start(bf16[32,192]{1,0:T(8,128)(2,1)S(1)} %collective-permute-done.8), channel_id=1, source_target_pairs={{1,0},{2,1},{3,2},{4,3},{5,4},{6,5},{7,6},{8,7},{9,8},{10,9},{11,1... | collective-permute-start | bytes 36872 | tf_op jit(solution)/shard_map/ppermute | solution.py:26
  45.4 4.5 %collective-permute-start.10 = (bf16[32,192]{1,0:T(8,128)(2,1)S(1)}, bf16[32,192]{1,0:T(8,128)(2,1)S(1)}, u32[]{:S(2)}, u32[]{:S(2)}) collective-permute-start(bf16[32,192]{1,0:T(8,128)(2,1)S(1)} %collective-permute-done.9), channel_id=1, source_target_pairs={{1,0},{2,1},{3,2},{4,3},{5,4},{6,5},{7,6},{8,7},{9,8},{10,9},{11,1... | collective-permute-start | bytes 36872 | tf_op jit(solution)/shard_map/ppermute | solution.py:26
  52.6 4.5 %collective-permute-start.11 = (bf16[32,192]{1,0:T(8,128)(2,1)S(1)}, bf16[32,192]{1,0:T(8,128)(2,1)S(1)}, u32[]{:S(2)}, u32[]{:S(2)}) collective-permute-start(bf16[32,192]{1,0:T(8,128)(2,1)S(1)} %collective-permute-done.10), channel_id=1, source_target_pairs={{1,0},{2,1},{3,2},{4,3},{5,4},{6,5},{7,6},{8,7},{9,8},{10,9},{11,1... | collective-permute-start | bytes 36872 | tf_op jit(solution)/shard_map/ppermute | solution.py:26
  57.1 1.4 collective-permute-done.11
  58.5 4.4 %collective-permute-start.12 = (bf16[32,192]{1,0:T(8,128)(2,1)S(1)}, bf16[32,192]{1,0:T(8,128)(2,1)S(1)}, u32[]{:S(2)}, u32[]{:S(2)}) collective-permute-start(bf16[32,192]{1,0:T(8,128)(2,1)S(1)} %collective-permute-done.11), channel_id=1, source_target_pairs={{1,0},{2,1},{3,2},{4,3},{5,4},{6,5},{7,6},{8,7},{9,8},{10,9},{11,1... | collective-permute-start | bytes 36872 | tf_op jit(solution)/shard_map/ppermute | solution.py:26
  62.9 1.4 collective-permute-done.12
  64.3 4.4 %collective-permute-start.13 = (bf16[32,192]{1,0:T(8,128)(2,1)S(1)}, bf16[32,192]{1,0:T(8,128)(2,1)S(1)}, u32[]{:S(2)}, u32[]{:S(2)}) collective-permute-start(bf16[32,192]{1,0:T(8,128)(2,1)S(1)} %collective-permute-done.12), channel_id=1, source_target_pairs={{1,0},{2,1},{3,2},{4,3},{5,4},{6,5},{7,6},{8,7},{9,8},{10,9},{11,1... | collective-permute-start | bytes 36872 | tf_op jit(solution)/shard_map/ppermute | solution.py:26
  70.7 4.5 %collective-permute-start.14 = (bf16[32,192]{1,0:T(8,128)(2,1)S(1)}, bf16[32,192]{1,0:T(8,128)(2,1)S(1)}, u32[]{:S(2)}, u32[]{:S(2)}) collective-permute-start(bf16[32,192]{1,0:T(8,128)(2,1)S(1)} %collective-permute-done.13), channel_id=1, source_target_pairs={{1,0},{2,1},{3,2},{4,3},{5,4},{6,5},{7,6},{8,7},{9,8},{10,9},{11,1... | collective-permute-start | bytes 36872 | tf_op jit(solution)/shard_map/ppermute | solution.py:26
  78.5 33.9 %all-reduce.1 = (f32[512,1]{0,1:T(1,128)S(1)}, f32[512]{0:T(512)S(1)}) all-reduce(f32[512,1]{0,1:T(1,128)S(1)} %convolution_bitcast_fusion.1, f32[512]{0:T(512)S(1)} %dynamic-update-slice.2), channel_id=1, replica_groups=mesh['groups'=2,'traj'=16] {'traj'}, use_global_device_ids=true, to_apply=%region_3.4 | all-reduce | flops 1024 | bytes 8192 | tf_op jit(solution)/shard_map/psum | solution.py:106
  113.2 1.7 fusion.21
  115.0 86.2 %all-reduce.5.cloned.1.call-done = f32[512,32]{1,0:T(8,128)} async-done(((f32[512,32]{1,0:T(8,128)}), f32[512,32]{1,0:T(8,128)}) %all-reduce.5.cloned.1.call-update) | async-done | bytes 65552 | tf_op jit(solution)/shard_map/psum | solution.py:106
  201.2 1.8 convolution_multiply_fusion.5
  203.4 60.0 %psum.37 = f32[32,32]{0,1:T(8,128)S(1)} all-reduce(f32[32,32]{0,1:T(8,128)S(1)} %rev.9), channel_id=1, replica_groups=mesh['groups'=2,'traj'=16] {'traj'}, use_global_device_ids=true, to_apply=%region_5.6 | all-reduce | flops 1024 | bytes 8192 | tf_op jit(solution)/shard_map/psum | solution.py:128
  263.4 2.9 cholesky.44
  267.7 2.5 custom-call.6
  270.5 1.7 fusion.19
  272.2 86.2 %all-reduce.7.cloned.1.call-done = f32[512,32]{1,0:T(8,128)} async-done(((f32[512,32]{1,0:T(8,128)}), f32[512,32]{1,0:T(8,128)}) %all-reduce.7.cloned.1.call-update) | async-done | bytes 65552 | tf_op jit(solution)/shard_map/psum | solution.py:106
  358.4 1.8 convolution_multiply_fusion.4
  360.4 60.0 %psum.39 = f32[32,32]{0,1:T(8,128)S(1)} all-reduce(f32[32,32]{0,1:T(8,128)S(1)} %fusion.42), channel_id=1, replica_groups=mesh['groups'=2,'traj'=16] {'traj'}, use_global_device_ids=true, to_apply=%region_9.12 | all-reduce | flops 1024 | bytes 8192 | tf_op jit(solution)/shard_map/psum | solution.py:134
  420.5 2.9 cholesky.55
  424.7 2.4 custom-call.7
  (89 shorter events, 17.4 us)
Async XLA Ops:
  6.5 194.7 %all-reduce.5.cloned.1.call-start = ((), (), s32[]{:S(2)}) async-start(), calls=%async_computation | async-start | bytes 524288 | tf_op jit(solution)/shard_map/psum | solution.py:106
  6.5 0.7 copy-start.2
  9.0 30.2 %collective-permute-start.8 = (bf16[32,192]{1,0:T(8,128)(2,1)S(1)}, bf16[32,192]{1,0:T(8,128)(2,1)S(1)}, u32[]{:S(2)}, u32[]{:S(2)}) collective-permute-start(bf16[32,192]{1,0:T(8,128)(2,1)S(1)} %broadcast_select_fusion), channel_id=1, source_target_pairs={{1,0},{2,1},{3,2},{4,3},{5,4},{6,5},{7,6},{8,7},{9,8},{10,9},{11,1... | collective-permute-start | bytes 36872 | tf_op jit(solution)/shard_map/ppermute | solution.py:26
  14.4 18.9 %collective-permute-start = (bf16[32,192]{1,0:T(8,128)(2,1)S(1)}, bf16[32,192]{1,0:T(8,128)(2,1)S(1)}, u32[]{:S(2)}, u32[]{:S(2)}) collective-permute-start(bf16[32,192]{1,0:T(8,128)(2,1)S(1)} %broadcast_select_fusion), channel_id=1, source_target_pairs={{0,1},{1,2},{2,3},{3,4},{4,5},{5,6},{6,7},{7,8},{8,9},{9,10},{10,1... | collective-permute-start | bytes 36872 | tf_op jit(solution)/shard_map/ppermute | solution.py:24
  33.3 5.9 %copy-start = (bf16[512,192]{0,1:T(8,128)(2,1)S(1)}, bf16[512,192]{0,1:T(8,128)(2,1)}, u32[]{:S(2)}) copy-start(bf16[512,192]{0,1:T(8,128)(2,1)} %param.6) | copy-start | bytes 589828
  33.3 5.9 %collective-permute-start.1 = (bf16[32,192]{1,0:T(8,128)(2,1)S(1)}, bf16[32,192]{1,0:T(8,128)(2,1)S(1)}, u32[]{:S(2)}, u32[]{:S(2)}) collective-permute-start(bf16[32,192]{1,0:T(8,128)(2,1)S(1)} %collective-permute-done), channel_id=1, source_target_pairs={{0,1},{1,2},{2,3},{3,4},{4,5},{5,6},{6,7},{7,8},{8,9},{9,10},{10,1... | collective-permute-start | bytes 36872 | tf_op jit(solution)/shard_map/ppermute | solution.py:24
  39.1 5.9 %collective-permute-start.2 = (bf16[32,192]{1,0:T(8,128)(2,1)S(1)}, bf16[32,192]{1,0:T(8,128)(2,1)S(1)}, u32[]{:S(2)}, u32[]{:S(2)}) collective-permute-start(bf16[32,192]{1,0:T(8,128)(2,1)S(1)} %collective-permute-done.1), channel_id=1, source_target_pairs={{0,1},{1,2},{2,3},{3,4},{4,5},{5,6},{6,7},{7,8},{8,9},{9,10},{10,1... | collective-permute-start | bytes 36872 | tf_op jit(solution)/shard_map/ppermute | solution.py:24
  39.2 6.2 %collective-permute-start.9 = (bf16[32,192]{1,0:T(8,128)(2,1)S(1)}, bf16[32,192]{1,0:T(8,128)(2,1)S(1)}, u32[]{:S(2)}, u32[]{:S(2)}) collective-permute-start(bf16[32,192]{1,0:T(8,128)(2,1)S(1)} %collective-permute-done.8), channel_id=1, source_target_pairs={{1,0},{2,1},{3,2},{4,3},{5,4},{6,5},{7,6},{8,7},{9,8},{10,9},{11,1... | collective-permute-start | bytes 36872 | tf_op jit(solution)/shard_map/ppermute | solution.py:26
  45.0 5.9 %collective-permute-start.3 = (bf16[32,192]{1,0:T(8,128)(2,1)S(1)}, bf16[32,192]{1,0:T(8,128)(2,1)S(1)}, u32[]{:S(2)}, u32[]{:S(2)}) collective-permute-start(bf16[32,192]{1,0:T(8,128)(2,1)S(1)} %collective-permute-done.2), channel_id=1, source_target_pairs={{0,1},{1,2},{2,3},{3,4},{4,5},{5,6},{6,7},{7,8},{8,9},{9,10},{10,1... | collective-permute-start | bytes 36872 | tf_op jit(solution)/shard_map/ppermute | solution.py:24
  45.4 7.2 %collective-permute-start.10 = (bf16[32,192]{1,0:T(8,128)(2,1)S(1)}, bf16[32,192]{1,0:T(8,128)(2,1)S(1)}, u32[]{:S(2)}, u32[]{:S(2)}) collective-permute-start(bf16[32,192]{1,0:T(8,128)(2,1)S(1)} %collective-permute-done.9), channel_id=1, source_target_pairs={{1,0},{2,1},{3,2},{4,3},{5,4},{6,5},{7,6},{8,7},{9,8},{10,9},{11,1... | collective-permute-start | bytes 36872 | tf_op jit(solution)/shard_map/ppermute | solution.py:26
  50.8 6.2 %collective-permute-start.4 = (bf16[32,192]{1,0:T(8,128)(2,1)S(1)}, bf16[32,192]{1,0:T(8,128)(2,1)S(1)}, u32[]{:S(2)}, u32[]{:S(2)}) collective-permute-start(bf16[32,192]{1,0:T(8,128)(2,1)S(1)} %collective-permute-done.3), channel_id=1, source_target_pairs={{0,1},{1,2},{2,3},{3,4},{4,5},{5,6},{6,7},{7,8},{8,9},{9,10},{10,1... | collective-permute-start | bytes 36872 | tf_op jit(solution)/shard_map/ppermute | solution.py:24
  52.6 5.9 %collective-permute-start.11 = (bf16[32,192]{1,0:T(8,128)(2,1)S(1)}, bf16[32,192]{1,0:T(8,128)(2,1)S(1)}, u32[]{:S(2)}, u32[]{:S(2)}) collective-permute-start(bf16[32,192]{1,0:T(8,128)(2,1)S(1)} %collective-permute-done.10), channel_id=1, source_target_pairs={{1,0},{2,1},{3,2},{4,3},{5,4},{6,5},{7,6},{8,7},{9,8},{10,9},{11,1... | collective-permute-start | bytes 36872 | tf_op jit(solution)/shard_map/ppermute | solution.py:26
  57.0 5.9 %collective-permute-start.5 = (bf16[32,192]{1,0:T(8,128)(2,1)S(1)}, bf16[32,192]{1,0:T(8,128)(2,1)S(1)}, u32[]{:S(2)}, u32[]{:S(2)}) collective-permute-start(bf16[32,192]{1,0:T(8,128)(2,1)S(1)} %collective-permute-done.4), channel_id=1, source_target_pairs={{0,1},{1,2},{2,3},{3,4},{4,5},{5,6},{6,7},{7,8},{8,9},{9,10},{10,1... | collective-permute-start | bytes 36872 | tf_op jit(solution)/shard_map/ppermute | solution.py:24
  58.5 5.9 %collective-permute-start.12 = (bf16[32,192]{1,0:T(8,128)(2,1)S(1)}, bf16[32,192]{1,0:T(8,128)(2,1)S(1)}, u32[]{:S(2)}, u32[]{:S(2)}) collective-permute-start(bf16[32,192]{1,0:T(8,128)(2,1)S(1)} %collective-permute-done.11), channel_id=1, source_target_pairs={{1,0},{2,1},{3,2},{4,3},{5,4},{6,5},{7,6},{8,7},{9,8},{10,9},{11,1... | collective-permute-start | bytes 36872 | tf_op jit(solution)/shard_map/ppermute | solution.py:26
  62.9 5.9 %collective-permute-start.6 = (bf16[32,192]{1,0:T(8,128)(2,1)S(1)}, bf16[32,192]{1,0:T(8,128)(2,1)S(1)}, u32[]{:S(2)}, u32[]{:S(2)}) collective-permute-start(bf16[32,192]{1,0:T(8,128)(2,1)S(1)} %collective-permute-done.5), channel_id=1, source_target_pairs={{0,1},{1,2},{2,3},{3,4},{4,5},{5,6},{6,7},{7,8},{8,9},{9,10},{10,1... | collective-permute-start | bytes 36872 | tf_op jit(solution)/shard_map/ppermute | solution.py:24
  64.3 6.3 %collective-permute-start.13 = (bf16[32,192]{1,0:T(8,128)(2,1)S(1)}, bf16[32,192]{1,0:T(8,128)(2,1)S(1)}, u32[]{:S(2)}, u32[]{:S(2)}) collective-permute-start(bf16[32,192]{1,0:T(8,128)(2,1)S(1)} %collective-permute-done.12), channel_id=1, source_target_pairs={{1,0},{2,1},{3,2},{4,3},{5,4},{6,5},{7,6},{8,7},{9,8},{10,9},{11,1... | collective-permute-start | bytes 36872 | tf_op jit(solution)/shard_map/ppermute | solution.py:26
  68.8 6.4 %collective-permute-start.7 = (bf16[32,192]{1,0:T(8,128)(2,1)S(1)}, bf16[32,192]{1,0:T(8,128)(2,1)S(1)}, u32[]{:S(2)}, u32[]{:S(2)}) collective-permute-start(bf16[32,192]{1,0:T(8,128)(2,1)S(1)} %collective-permute-done.6), channel_id=1, source_target_pairs={{0,1},{1,2},{2,3},{3,4},{4,5},{5,6},{6,7},{7,8},{8,9},{9,10},{10,1... | collective-permute-start | bytes 36872 | tf_op jit(solution)/shard_map/ppermute | solution.py:24
  68.8 0.7 copy-start.3
  70.7 5.9 %collective-permute-start.14 = (bf16[32,192]{1,0:T(8,128)(2,1)S(1)}, bf16[32,192]{1,0:T(8,128)(2,1)S(1)}, u32[]{:S(2)}, u32[]{:S(2)}) collective-permute-start(bf16[32,192]{1,0:T(8,128)(2,1)S(1)} %collective-permute-done.13), channel_id=1, source_target_pairs={{1,0},{2,1},{3,2},{4,3},{5,4},{6,5},{7,6},{8,7},{9,8},{10,9},{11,1... | collective-permute-start | bytes 36872 | tf_op jit(solution)/shard_map/ppermute | solution.py:26
  112.4 0.8 copy-start.1
  114.9 243.5 %all-reduce.7.cloned.1.call-start = ((), (), s32[]{:S(2)}) async-start(), calls=%async_computation.1 | async-start | bytes 524288 | tf_op jit(solution)/shard_map/psum | solution.py:106
Sparse Core Ops, SparseCore 0:
  115.1 86.1 all-reduce.4
  272.3 86.0 all-reduce.6
